TPU v7x, 768 devices: a whole 4x8x12 slice. The times are simulated.
768 devices in a mesh: vir: 64 (over x, y, core), occ: 12 (over z).
Axes of the slice: x: 4, y: 8, z: 12, core: 2. Of those that a mesh axis runs over, the one named last changes fastest.
Arguments:
- amps: bfloat16 [64, 768, 4096], P('vir'), may hold values from -6 to 6
- ints: bfloat16 [64, 36, 4096, 128], P('vir', 'occ'), may hold values from -0.015625 to 0.015625
- partners: int32 [64, 36], P('vir'), may hold values from 0 to 63, as said below
- irrep_sizes: int32 [2], replicated, may hold values from 31 to 33, as said below
- tile_slot: int32 [64], replicated, may hold values from 0 to 63, as said below
Outputs:
- residual: float32 [64, 768, 128], P('vir', 'occ')
Inputs may be any that keep to these rules, and one draw needn't show every extreme that they name: `partners`: row s belongs to the tile at slot s: its first n entries, n being the size of that tile's irrep block, are the distinct tile ids of that block in some order; the remaining entries are distinct ids of the other block and name no allowed triple. A tile id is in block 0 if it is below irrep_sizes[0], else in block 1. `irrep_sizes`: one of the two sizes is 33 and the other is 31, in either order. A permutation: tile id t sits at slot tile_slot[t], the index along the first dimension of amps, ints, partners and residual.
All inputs are finite; a program needn't handle non-finite values.
Results may differ from a plain program's by a relative error of at most 0.0003.
Values sent between devices are 32-bit elements; how exact they have to be, the bound alone decides.
No kernel may reach another device: no remote copies, remote signals or barrier semaphores. Data moves between devices by JAX's collectives and lax.ppermute only.
A program may use at most 128 MiB of HBM per device.

v0:
```python
import jax
import jax.numpy as jnp
from jax import lax
from jax.sharding import PartitionSpec as P


def shards(amps, ints, partners, irrep_sizes, tile_slot):
    tile_count = tile_slot.shape[0]
    slot_count = ints.shape[1]
    my_slot = lax.axis_index("vir")
    tile_ids = jnp.arange(tile_count, dtype=jnp.int32)
    own_tile = jnp.sum(jnp.where(tile_slot == my_slot, tile_ids, 0))
    live_count = jnp.where(own_tile >= irrep_sizes[0], irrep_sizes[1], irrep_sizes[0])
    partner_ids = partners[0]
    targets = jnp.sum(
        jnp.where(partner_ids[:, None] == tile_ids[None, :], tile_slot[None, :], 0), axis=1
    )
    slot_order = jnp.arange(partner_ids.shape[0], dtype=jnp.int32)
    live_slots = slot_order < live_count
    first_slot = lax.axis_index("occ") * slot_count
    my_live = lax.dynamic_slice_in_dim(live_slots, first_slot, slot_count)
    products = jnp.einsum("ic,kcr->kir", amps[0], ints[0], preferred_element_type=jnp.float32)
    products = jnp.where(my_live[:, None, None], products, jnp.float32(0.0))
    my_targets = lax.dynamic_slice_in_dim(targets, first_slot, slot_count)
    scattered = (
        jnp.zeros((tile_count,) + products.shape[1:], jnp.float32).at[my_targets].add(products)
    )
    tile_totals = lax.psum_scatter(scattered, "vir", scatter_dimension=0, tiled=True)
    residual = lax.psum_scatter(tile_totals, "occ", scatter_dimension=1, tiled=True)
    return residual


def solution(mesh):
    in_specs = (P("vir", None, None), P("vir", "occ", None, None), P("vir", None), P(), P())
    out_specs = P("vir", "occ", None)
    return jax.shard_map(shards, mesh=mesh, in_specs=in_specs, out_specs=out_specs, check_vma=False)
```

profile of v0, /device:TPU:4, one launch (start us, length us, event | category | flops | bytes accessed | tf_op | source)
XLA Modules:
  0.0 346.6 jit_solution(2528545593553438904)
XLA Ops:
  6.5 0.0 copy-start
  6.5 0.0 reduce-scatter.3.cloned.1.call-start
  6.5 1.4 fusion.13
  8.0 0.8 select_reduce_fusion
  8.8 1.4 fusion.14
  12.7 0.1 compare_select_fusion
  12.8 0.1 dynamic_slice.7
  12.9 0.0 copy-done
  12.9 6.4 %fusion.8 = f32[3,768,128]{1,2,0:T(8,128)} fusion(bf16[1,768,4096]{2,1,0:T(8,128)(2,1)} %param.5, bf16[1,3,4096,128]{3,2,1,0:T(8,128)(2,1)S(1)} %copy-done, pred[3]{0:T(512)(128)(4,1)S(1)} %dynamic_slice.7), kind=kOutput, calls=%fused_computation.5 | convolution fusion | flops 2416214016 | bytes 10616835 | tf_op jit(solution)/shard_map/ic,kcr->kir/dot_general | solution.py:22
  19.3 2.7 copy.9
  22.1 11.4 %broadcast_in_dim.37 = f32[64,768,128]{2,1,0:T(8,128)} broadcast(f32[]{:T(128)} %constant.7.clone.1), dimensions={} | broadcast | bytes 25165828 | tf_op jit(solution)/shard_map/broadcast_in_dim | solution.py:26
  33.5 3.8 %scatter_fusion = f32[64,768,128]{2,1,0:T(8,128)} fusion(f32[64,768,128]{2,1,0:T(8,128)} %broadcast_in_dim.37, s32[3]{0:T(128)S(1)} %compare_select_fusion, f32[3,768,128]{2,1,0:T(8,128)} %copy.9), kind=kCustom, calls=%fused_computation | custom fusion | flops 294912 | bytes 3538956 | tf_op jit(solution)/shard_map/scatter-add | solution.py:26
  37.2 0.0 reduce-scatter.3.cloned.1.call-update
  37.3 0.0 reduce-scatter.5.cloned.1.call-start
  37.3 242.8 %reduce-scatter.3.cloned.1.call-done = f32[1,768,128]{2,1,0:T(8,128)} async-done(((f32[64,768,128]{2,1,0:T(8,128)}), f32[1,768,128]{2,1,0:T(8,128)}) %reduce-scatter.3.cloned.1.call-update) | async-done | bytes 393232 | tf_op jit(solution)/shard_map/reduce_scatter | solution.py:28
  280.1 0.0 reduce-scatter.5.cloned.1.call-update
  280.1 59.6 %reduce-scatter.5.cloned.1.call-done = f32[1,64,128]{2,1,0:T(8,128)} async-done(((f32[1,768,128]{2,1,0:T(8,128)}), f32[1,64,128]{2,1,0:T(8,128)}) %reduce-scatter.5.cloned.1.call-update) | async-done | bytes 32784 | tf_op jit(solution)/shard_map/reduce_scatter | solution.py:29
  (1 shorter events, 0.0 us)
Async XLA Ops:
  6.5 6.3 %copy-start = (bf16[1,3,4096,128]{3,2,1,0:T(8,128)(2,1)S(1)}, bf16[1,3,4096,128]{3,2,1,0:T(8,128)(2,1)}, u32[]{:S(2)}) copy-start(bf16[1,3,4096,128]{3,2,1,0:T(8,128)(2,1)} %param.6) | copy-start | bytes 9437188
  6.5 273.6 %reduce-scatter.3.cloned.1.call-start = ((), (), s32[]{:S(2)}) async-start(), calls=%async_computation.2 | async-start | bytes 25559040 | tf_op jit(solution)/shard_map/reduce_scatter | solution.py:28
  37.3 302.5 %reduce-scatter.5.cloned.1.call-start = ((), (), s32[]{:S(2)}) async-start(), calls=%async_computation.3 | async-start | bytes 425984 | tf_op jit(solution)/shard_map/reduce_scatter | solution.py:29
Sparse Core Ops, SparseCore 0:
  37.4 242.6 reduce-scatter.2
  283.2 56.5 reduce-scatter.4
where the time goes:
time: 347 us
  waiting for transfers between devices  302 us (87%)
  between operations  15.9 us (5%)
  local copies, waits for them, and re-layouts  15.6 us (4%)
  matrix products  6.45 us (2%)
  other arithmetic  6.15 us (2%)
    reduce_scatter x1, waiting for transfers between devices, shards(): lax.psum_scatter(scattered, 'vir', scatter_dimension=0, tiled=True)  243 us
    reduce_scatter x1, waiting for transfers between devices, shards(): lax.psum_scatter(tile_totals, 'occ', scatter_dimension=1, tiled=True)  59.6 us
    broadcast_in_dim x1, local copies, waits for them, and re-layouts, shards(): jnp.zeros((tile_count,) + products.shape[1:], jnp.float32).at[my_targets]  11.4 us
  transfers between devices with their start and end apart: 2, of which 2 were waited for; matrix products, arithmetic and copies ran while one was open for 0% of the time, Pallas kernels for 0%

commit v1 on v0

v1 whole, which is shorter than its diff:
```python
import jax
import jax.numpy as jnp
from jax import lax
from jax.experimental import pallas as pl
from jax.experimental.pallas import tpu as pltpu
from jax.sharding import Mesh
from jax.sharding import PartitionSpec as P

TILES = 64
PLANES = 12
GROUP = 4
HEADS = PLANES // GROUP
PER = 3
LINES = PER * HEADS + 1
FIRST = TILES * GROUP
SECOND = TILES * HEADS
LANES = 128
CHUNK = 512
VIR = ("x", "y", "core")


def codes_row(place, sizes, slots, partners):
    slot, plane = place[0], place[1]
    own = lax.fori_loop(
        0, TILES, lambda t, own: own + jnp.where(slots[t] == slot, t, 0), jnp.int32(0)
    )
    live = jnp.where(own >= sizes[0], sizes[1], sizes[0])
    lanes = lax.broadcasted_iota(jnp.int32, (1, LANES), 1)
    row = jnp.zeros((1, LANES), jnp.float32)
    for k in range(PER):
        index = plane * PER + k
        target = jnp.where(index < live, slots[partners[index]], -1)
        row = jnp.where(lanes == target, jnp.float32(k + 1), row)
    return row


def products_kernel(place, sizes, slots, partners, amps, ints, out, total):
    step = pl.program_id(0)
    weights = jnp.concatenate([ints[k] for k in range(PER)], axis=1)
    part = jnp.dot(amps[...], weights, preferred_element_type=jnp.float32)

    @pl.when(step == 0)
    def _():
        total[...] = part

    @pl.when(step > 0)
    def _():
        total[...] += part

    @pl.when(step == pl.num_programs(0) - 1)
    def _():
        for head in range(HEADS):
            for near in range(GROUP):
                rows = pl.ds(TILES * (head * GROUP + near), TILES)
                for k in range(PER):
                    line = near * LINES + k * HEADS + head
                    out[pl.ds(line, TILES, stride=GROUP * LINES), :] = total[
                        rows, k * LANES : (k + 1) * LANES
                    ]
        row = codes_row(place, sizes, slots, partners)
        out[pl.ds(LINES - 1, FIRST, stride=LINES), :] = jnp.broadcast_to(row, (FIRST, LANES))


def products(place, sizes, slots, partners, amps, ints):
    pairs, depth = amps.shape
    scalars = pl.BlockSpec(memory_space=pltpu.SMEM)
    return pl.pallas_call(
        products_kernel,
        grid=(depth // CHUNK,),
        in_specs=[
            scalars,
            scalars,
            scalars,
            scalars,
            pl.BlockSpec((pairs, CHUNK), lambda i: (0, i)),
            pl.BlockSpec((PER, CHUNK, LANES), lambda i: (0, i, 0)),
        ],
        out_specs=pl.BlockSpec((FIRST * LINES, LANES), lambda i: (0, 0)),
        out_shape=jax.ShapeDtypeStruct((FIRST * LINES, LANES), jnp.float32),
        scratch_shapes=[pltpu.VMEM((pairs, PER * LANES), jnp.float32)],
        compiler_params=pltpu.CompilerParams(vmem_limit_bytes=56 * 1024 * 1024),
        name="products",
    )(place, sizes, slots, partners, amps, ints)


def gather_kernel(got, out):
    codes = jnp.transpose(got[pl.ds(LINES - 1, FIRST, stride=LINES), :])[:TILES]
    picks = [(codes == jnp.float32(k + 1)).astype(jnp.bfloat16) for k in range(PER)]
    for head in range(HEADS):
        sums = jnp.zeros((TILES, LANES), jnp.float32)
        for k in range(PER):
            rows = got[pl.ds(k * HEADS + head, FIRST, stride=LINES), :]
            high = rows.astype(jnp.bfloat16)
            rest = rows - high.astype(jnp.float32)
            middle = rest.astype(jnp.bfloat16)
            low = (rest - middle.astype(jnp.float32)).astype(jnp.bfloat16)
            for term in (low, middle, high):
                sums += jnp.dot(picks[k], term, preferred_element_type=jnp.float32)
        out[pl.ds(head, TILES, stride=HEADS), :] = sums


def gather(got):
    return pl.pallas_call(
        gather_kernel,
        out_shape=jax.ShapeDtypeStruct((SECOND, LANES), jnp.float32),
        compiler_params=pltpu.CompilerParams(vmem_limit_bytes=56 * 1024 * 1024),
        name="gather",
    )(got)


def finish_kernel(got, out):
    out[...] = sum(got[pl.ds(head, TILES, stride=HEADS), :] for head in range(HEADS))


def finish(got):
    return pl.pallas_call(
        finish_kernel,
        out_shape=jax.ShapeDtypeStruct((TILES, LANES), jnp.float32),
        name="finish",
    )(got)


def shards(amps, ints, partners, irrep_sizes, tile_slot):
    place = jnp.stack([lax.axis_index(VIR), lax.axis_index(("far", "near"))]).astype(jnp.int32)
    sent = products(place, irrep_sizes, tile_slot, partners[0], amps[0], ints[0])
    got = lax.all_to_all(
        sent.reshape(FIRST, LINES, 1, LANES), VIR + ("near",), 0, 0, tiled=True
    )
    sums = gather(got.reshape(FIRST * LINES, LANES))
    got = lax.all_to_all(sums.reshape(SECOND, 1, LANES), VIR + ("far",), 0, 0, tiled=True)
    return finish(got.reshape(SECOND, LANES))[None]


def solution(mesh):
    fine = Mesh(
        mesh.devices.reshape(4, 8, 2, HEADS, GROUP), ("x", "y", "core", "far", "near")
    )
    occ = ("far", "near")
    in_specs = (P(VIR, None, None), P(VIR, occ, None, None), P(VIR, None), P(), P())
    out_specs = P(VIR, occ, None)
    return jax.shard_map(shards, mesh=fine, in_specs=in_specs, out_specs=out_specs, check_vma=False)
```

time: 347 us -> 102 us (0.29)
  the two profiles are of different devices: /device:TPU:4 before, /device:TPU:1 now
where the time goes in v1:
time: 102 us
  blocking collectives  86.5 us (85%)
  Pallas kernels  14.7 us (14%)
    all_to_all x1, blocking collectives, shards(): lax.all_to_all(sent.reshape(FIRST, LINES, 1, LANES), VIR + ('near',), 0,...  56.9 us
    all_to_all x1, blocking collectives, shards(): lax.all_to_all(sums.reshape(SECOND, 1, LANES), VIR + ('far',), 0, 0, tile...  29.6 us
    pallas_call x1, Pallas kernels, products(): pl.pallas_call(products_kernel, grid=(depth // CHUNK,), in_specs=[scalars...  10.8 us
    pallas_call x1, Pallas kernels, gather(): pl.pallas_call(gather_kernel, out_shape=jax.ShapeDtypeStruct((SECOND, LAN...  2.41 us

profile of v1, /device:TPU:1, one launch (start us, length us, event | category | flops | bytes accessed | tf_op | source)
XLA Modules:
  0.0 101.8 jit_solution(17011765303447158972)
XLA Ops:
  0.0 0.6 pad_add_fusion.place
  0.6 10.8 %products.1 = f32[2560,128]{1,0:T(8,128)} custom-call(s32[2]{0:T(128)} %pad_add_fusion.place, s32[2]{0:T(128)} %sizes.1, s32[64]{0:T(128)} %slots.1, s32[36]{0:T(128)} %bitcast.18, bf16[768,4096]{1,0:T(8,128)(2,1)} %bitcast.12, bf16[3,4096,128]{2,1,0:T(8,128)(2,1)} %bitcast.15), custom_call_target="tpu_custom_call" | custom-call | tf_op jit(solution)/shard_map/products/pallas_call | solution.py:67
  11.4 56.9 %all_to_all.10 = f32[256,10,1,128]{3,2,1,0:T(1,128)} all-to-all(f32[256,10,1,128]{3,2,1,0:T(1,128)} %bitcast.14), channel_id=1, replica_groups=mesh['x'=4,'y'=8,'core'=2,'far'=3,'near'=4] {'x','y','core','near'}, dimensions={0} | all-to-all | bytes 2621440 | tf_op jit(solution)/shard_map/all_to_all | solution.py:126
  68.3 2.4 %gather.1 = f32[192,128]{1,0:T(8,128)} custom-call(f32[2560,128]{1,0:T(8,128)} %bitcast.13), custom_call_target="tpu_custom_call" | custom-call | tf_op jit(solution)/shard_map/gather/pallas_call | solution.py:103
  70.7 29.6 %all_to_all.11 = f32[192,1,128]{2,1,0:T(1,128)} all-to-all(f32[192,1,128]{2,1,0:T(1,128)} %bitcast.17), channel_id=1, replica_groups=mesh['x'=4,'y'=8,'core'=2,'far'=3,'near'=4] {'x','y','core','far'}, dimensions={0} | all-to-all | bytes 196608 | tf_op jit(solution)/shard_map/all_to_all | solution.py:130
  100.3 1.5 %finish.1 = f32[64,128]{1,0:T(8,128)} custom-call(f32[192,128]{1,0:T(8,128)} %bitcast.16), custom_call_target="tpu_custom_call" | custom-call | tf_op jit(solution)/shard_map/finish/pallas_call | solution.py:116

commit v2 on v0

v2 whole, which is shorter than its diff:
```python
import jax
import jax.numpy as jnp
from jax import lax
from jax.experimental import pallas as pl
from jax.experimental.pallas import tpu as pltpu
from jax.sharding import Mesh
from jax.sharding import PartitionSpec as P

TILES = 64
PLANES = 12
NEAR_Y = 2
NEAR_Z = 3
FAR_Y = 8 // NEAR_Y
FAR_Z = PLANES // NEAR_Z
PER = 3
PIECES = 8 * NEAR_Y
EACH = TILES // PIECES
FIRST = PIECES * NEAR_Z
THIRD = PIECES * FAR_Z
PARTS = FAR_Y * FAR_Z
LINES = PER * FAR_Z * EACH + 1
LANES = 128
CHUNK = 512
HALF = 384
ROOM = 56 * 1024 * 1024
SMALL = 16 * 1024 * 1024
VIR = ("x", "far_y", "near_y", "core")
OCC = ("far_z", "near_z")


def codes_row(sizes, slots, partners):
    y = lax.axis_index("far_y") * NEAR_Y + lax.axis_index("near_y")
    slot = (lax.axis_index("x") * 8 + y) * 2 + lax.axis_index("core")
    plane = lax.axis_index("far_z") * NEAR_Z + lax.axis_index("near_z")
    own = lax.fori_loop(
        0, TILES, lambda t, own: own + jnp.where(slots[t] == slot, t, 0), jnp.int32(0)
    )
    live = jnp.where(own >= sizes[0], sizes[1], sizes[0])
    lanes = lax.broadcasted_iota(jnp.int32, (1, LANES), 1)
    far, piece = lanes // PIECES, lanes % PIECES
    x, low = piece // (2 * NEAR_Y), piece % (2 * NEAR_Y)
    slot_of = (x * FAR_Y + far) * 2 * NEAR_Y + low
    slot_of = jnp.where(lanes < TILES, slot_of, -2)
    row = jnp.zeros((1, LANES), jnp.float32)
    for k in range(PER):
        index = plane * PER + k
        target = jnp.where(index < live, slots[partners[index]], -1)
        row = jnp.where(slot_of == target, jnp.float32(k + 1), row)
    return row


def products_kernel(sizes, slots, partners, amps, ints, out, left, right, total, sems):
    depth = amps.shape[1]
    copies = []
    for step in range(depth // CHUNK):
        part = pl.ds(step * CHUNK, CHUNK)
        copies.append(
            (
                pltpu.make_async_copy(amps.at[:, part], left.at[:, part], sems.at[0, step]),
                pltpu.make_async_copy(ints.at[:, part], right.at[:, part], sems.at[1, step]),
            )
        )
    for pair in copies:
        for copy in pair:
            copy.start()
    row = codes_row(sizes, slots, partners)
    out[pl.ds(LINES - 1, FIRST, stride=LINES), :] = jnp.broadcast_to(row, (FIRST, LANES))
    for step, pair in enumerate(copies):
        for copy in pair:
            copy.wait()
        part = pl.ds(step * CHUNK, CHUNK)
        weights = jnp.concatenate([right[k, part, :] for k in range(PER)], axis=1)
        for half in range(2):
            rows = pl.ds(half * HALF, HALF)
            now = jnp.dot(left[rows, part], weights, preferred_element_type=jnp.float32)
            for k in range(PER):
                term = now[:, k * LANES : (k + 1) * LANES]
                total[k, rows, :] = term if step == 0 else total[k, rows, :] + term
    for far in range(FAR_Z):
        for near in range(NEAR_Z):
            for k in range(PER):
                for j in range(EACH):
                    start = TILES * (far * NEAR_Z + near) + j
                    line = near * LINES + (k * FAR_Z + far) * EACH + j
                    out[pl.ds(line, PIECES, stride=NEAR_Z * LINES), :] = total[
                        k, pl.ds(start, PIECES, stride=EACH), :
                    ]


def products(sizes, slots, partners, amps, ints):
    pairs, depth = amps.shape
    scalars = pl.BlockSpec(memory_space=pltpu.SMEM)
    return pl.pallas_call(
        products_kernel,
        in_specs=[scalars] * 3 + [pl.BlockSpec(memory_space=pl.ANY)] * 2,
        out_specs=pl.BlockSpec(memory_space=pltpu.VMEM),
        out_shape=jax.ShapeDtypeStruct((FIRST * LINES, LANES), jnp.float32),
        scratch_shapes=[
            pltpu.VMEM((pairs, depth), jnp.bfloat16),
            pltpu.VMEM((PER, depth, LANES), jnp.bfloat16),
            pltpu.VMEM((PER, pairs, LANES), jnp.float32),
            pltpu.SemaphoreType.DMA((2, depth // CHUNK)),
        ],
        compiler_params=pltpu.CompilerParams(vmem_limit_bytes=ROOM),
        name="products",
    )(sizes, slots, partners, amps, ints)


def gather_kernel(got, out):
    codes = jnp.transpose(got[pl.ds(LINES - 1, FIRST, stride=LINES), :])[:TILES]
    picks = [(codes == jnp.float32(k + 1)).astype(jnp.float32) for k in range(PER)]
    picks = jnp.concatenate(picks * 3, axis=1).astype(jnp.bfloat16)
    for far in range(FAR_Z):
        for j in range(EACH):
            rows = [
                got[pl.ds((k * FAR_Z + far) * EACH + j, FIRST, stride=LINES), :]
                for k in range(PER)
            ]
            rows = jnp.concatenate(rows, axis=0)
            high = rows.astype(jnp.bfloat16)
            rest = rows - high.astype(jnp.float32)
            middle = rest.astype(jnp.bfloat16)
            low = (rest - middle.astype(jnp.float32)).astype(jnp.bfloat16)
            terms = jnp.concatenate([low, middle, high], axis=0)
            sums = jnp.dot(picks, terms, preferred_element_type=jnp.float32)
            for far_y in range(FAR_Y):
                start = (far_y * FAR_Z + far) * TILES + j
                out[pl.ds(start, PIECES, stride=EACH), :] = sums[
                    far_y * PIECES : (far_y + 1) * PIECES
                ]


def gather(got):
    return pl.pallas_call(
        gather_kernel,
        out_shape=jax.ShapeDtypeStruct((PARTS * TILES, LANES), jnp.float32),
        compiler_params=pltpu.CompilerParams(vmem_limit_bytes=SMALL),
        name="gather",
    )(got)


def add_kernel(got, out):
    rows = out.shape[0]
    out[...] = sum(got[pl.ds(start, rows), :] for start in range(0, got.shape[0], rows))


def add(got, parts):
    return pl.pallas_call(
        add_kernel,
        out_shape=jax.ShapeDtypeStruct((got.shape[0] // parts, LANES), jnp.float32),
        compiler_params=pltpu.CompilerParams(vmem_limit_bytes=SMALL),
        name="add",
    )(got)


def exchange(rows, axes, devices):
    each = rows.shape[0] // devices
    sent = rows.reshape(devices, each, 1, LANES)
    return lax.all_to_all(sent, axes, 0, 0, tiled=True).reshape(rows.shape)


def shards(amps, ints, partners, irrep_sizes, tile_slot):
    sent = products(irrep_sizes, tile_slot, partners[0], amps[0], ints[0])
    got = exchange(sent, ("x", "near_y", "core", "near_z"), FIRST)
    sums = gather(got)
    sums = add(exchange(sums, ("far_y",), FAR_Y), FAR_Y)
    got = exchange(sums, ("far_z", "x", "near_y", "core"), THIRD)
    return add(got, FAR_Z)[None]


def solution(mesh):
    fine = Mesh(mesh.devices.reshape(4, FAR_Y, NEAR_Y, 2, FAR_Z, NEAR_Z), VIR + OCC)
    in_specs = (P(VIR, None, None), P(VIR, OCC, None, None), P(VIR, None), P(), P())
    out_specs = P(VIR, OCC, None)
    return jax.shard_map(shards, mesh=fine, in_specs=in_specs, out_specs=out_specs, check_vma=False)
```

time: 347 us -> 94.9 us (0.27)
  the two profiles are of different devices: /device:TPU:4 before, /device:TPU:1 now
where the time goes in v2:
time: 94.9 us; the launch traced here: 94.6 us
  blocking collectives  86.4 us (91%)
  Pallas kernels  8.2 us (9%)
    all_to_all x3, blocking collectives, exchange(): return lax.all_to_all(sent, axes, 0, 0, tiled=True).reshape(rows.shape)  86.4 us
    pallas_call x1, Pallas kernels, products(): pl.pallas_call(products_kernel, in_specs=[scalars] * 3 + [pl.BlockSpec(me...  6.92 us

profile of v2, /device:TPU:1, one launch (start us, length us, event | category | flops | bytes accessed | tf_op | source)
XLA Modules:
  0.0 94.6 jit_solution(15055201078422383000)
XLA Ops:
  0.0 6.9 %products.1 = f32[2352,128]{1,0:T(8,128)} custom-call(s32[2]{0:T(128)} %sizes.1, s32[64]{0:T(128)} %slots.1, s32[36]{0:T(128)} %bitcast.22, bf16[768,4096]{1,0:T(8,128)(2,1)} %bitcast.19, bf16[3,4096,128]{2,1,0:T(8,128)(2,1)} %bitcast.21), custom_call_target="tpu_custom_call" | custom-call | tf_op jit(solution)/shard_map/products/pallas_call | solution.py:93
  6.9 38.5 %all_to_all.15 = f32[48,49,1,128]{3,2,1,0:T(1,128)S(1)} all-to-all(f32[48,49,1,128]{3,2,1,0:T(1,128)} %bitcast.20), channel_id=1, replica_groups=mesh['x'=4,'far_y'=4,'near_y'=2,'core'=2,'far_z'=4,'near_z'=3] {'x','nea..., dimensions={0} | all-to-all | bytes 2408448 | tf_op jit(solution)/shard_map/all_to_all | solution.py:159
  45.5 0.6 gather.1
  46.1 19.6 %all_to_all.16 = f32[4,256,1,128]{3,1,2,0:T(8,128)S(1)} all-to-all(f32[4,256,1,128]{3,1,2,0:T(8,128)S(1)} %bitcast.16), channel_id=1, replica_groups=mesh['x'=4,'far_y'=4,'near_y'=2,'core'=2,'far_z'=4,'near_z'=3] {'far_y'}, dimensions={0} | all-to-all | bytes 1048576 | tf_op jit(solution)/shard_map/all_to_all | solution.py:159
  65.8 28.2 %all_to_all.17 = f32[64,4,1,128]{3,1,2,0:T(4,128)S(1)} all-to-all(f32[64,4,1,128]{3,1,2,0:T(4,128)S(1)} %bitcast.17), channel_id=1, replica_groups=mesh['x'=4,'far_y'=4,'near_y'=2,'core'=2,'far_z'=4,'near_z'=3] {'far_z',..., dimensions={0} | all-to-all | bytes 262144 | tf_op jit(solution)/shard_map/all_to_all | solution.py:159
  94.0 0.6 add.3
  (1 shorter events, 0.0 us)

commit v3 on v2

--- a/solution.py
+++ b/solution.py
@@ -16,7 +16,6 @@
 PIECES = 8 * NEAR_Y
 EACH = TILES // PIECES
 FIRST = PIECES * NEAR_Z
-THIRD = PIECES * FAR_Z
 PARTS = FAR_Y * FAR_Z
 LINES = PER * FAR_Z * EACH + 1
 LANES = 128
@@ -140,14 +139,13 @@
 
 
 def add_kernel(got, out):
-    rows = out.shape[0]
-    out[...] = sum(got[pl.ds(start, rows), :] for start in range(0, got.shape[0], rows))
+    out[...] = sum(got[pl.ds(part * TILES, TILES), :] for part in range(PARTS))
 
 
-def add(got, parts):
+def add(got):
     return pl.pallas_call(
         add_kernel,
-        out_shape=jax.ShapeDtypeStruct((got.shape[0] // parts, LANES), jnp.float32),
+        out_shape=jax.ShapeDtypeStruct((TILES, LANES), jnp.float32),
         compiler_params=pltpu.CompilerParams(vmem_limit_bytes=SMALL),
         name="add",
     )(got)
@@ -163,9 +161,8 @@
     sent = products(irrep_sizes, tile_slot, partners[0], amps[0], ints[0])
     got = exchange(sent, ("x", "near_y", "core", "near_z"), FIRST)
     sums = gather(got)
-    sums = add(exchange(sums, ("far_y",), FAR_Y), FAR_Y)
-    got = exchange(sums, ("far_z", "x", "near_y", "core"), THIRD)
-    return add(got, FAR_Z)[None]
+    sums = add(exchange(sums, ("far_y", "far_z"), PARTS))
+    return exchange(sums, ("x", "near_y", "core"), PIECES)[None]
 
 
 def solution(mesh):

time: 94.9 us -> 97.6 us (1.028)
  blocking collectives: 86.4 us -> 89.1 us
    all_to_all x3, blocking collectives: 86.4 us -> 89.1 us  [exchange(): return lax.all_to_all(sent, axes, 0, 0, tiled=True).reshape(rows.shape)]
where the time goes in v3:
time: 97.6 us; the launch traced here: 97.3 us
  blocking collectives  89.1 us (91%)
  Pallas kernels  7.58 us (8%)
    all_to_all x3, blocking collectives, exchange(): return lax.all_to_all(sent, axes, 0, 0, tiled=True).reshape(rows.shape)  89.1 us
    pallas_call x1, Pallas kernels, products(): pl.pallas_call(products_kernel, in_specs=[scalars] * 3 + [pl.BlockSpec(me...  6.92 us

profile of v3, /device:TPU:1, one launch (start us, length us, event | category | flops | bytes accessed | tf_op | source)
XLA Modules:
  0.0 97.3 jit_solution(7869296958529520572)
XLA Ops:
  0.0 6.9 %products.1 = f32[2352,128]{1,0:T(8,128)} custom-call(s32[2]{0:T(128)} %sizes.1, s32[64]{0:T(128)} %slots.1, s32[36]{0:T(128)} %bitcast.21, bf16[768,4096]{1,0:T(8,128)(2,1)} %bitcast.17, bf16[3,4096,128]{2,1,0:T(8,128)(2,1)} %bitcast.19), custom_call_target="tpu_custom_call" | custom-call | tf_op jit(solution)/shard_map/products/pallas_call | solution.py:92
  6.9 38.5 %all_to_all.15 = f32[48,49,1,128]{3,2,1,0:T(1,128)S(1)} all-to-all(f32[48,49,1,128]{3,2,1,0:T(1,128)} %bitcast.18), channel_id=1, replica_groups=mesh['x'=4,'far_y'=4,'near_y'=2,'core'=2,'far_z'=4,'near_z'=3] {'x','nea..., dimensions={0} | all-to-all | bytes 2408448 | tf_op jit(solution)/shard_map/all_to_all | solution.py:157
  45.5 0.6 gather.1
  46.1 41.0 %all_to_all.16 = f32[16,64,1,128]{3,1,2,0:T(8,128)S(1)} all-to-all(f32[16,64,1,128]{3,1,2,0:T(8,128)S(1)} %bitcast.14), channel_id=1, replica_groups=mesh['x'=4,'far_y'=4,'near_y'=2,'core'=2,'far_z'=4,'near_z'=3] {'far_y',..., dimensions={0} | all-to-all | bytes 1048576 | tf_op jit(solution)/shard_map/all_to_all | solution.py:157
  87.1 9.6 %all_to_all.17 = f32[16,4,1,128]{3,1,2,0:T(4,128)S(1)} all-to-all(f32[16,4,1,128]{3,1,2,0:T(4,128)S(1)} %bitcast.16), channel_id=1, replica_groups=mesh['x'=4,'far_y'=4,'near_y'=2,'core'=2,'far_z'=4,'near_z'=3] {'x','nea..., dimensions={0} | all-to-all | bytes 65536 | tf_op jit(solution)/shard_map/all_to_all | solution.py:157
  96.7 0.6 copy.10
  (1 shorter events, 0.0 us)

commit v4 on v3

--- a/solution.py
+++ b/solution.py
@@ -16,7 +16,6 @@
 PIECES = 8 * NEAR_Y
 EACH = TILES // PIECES
 FIRST = PIECES * NEAR_Z
-PARTS = FAR_Y * FAR_Z
 LINES = PER * FAR_Z * EACH + 1
 LANES = 128
 CHUNK = 512
@@ -122,30 +121,38 @@
             low = (rest - middle.astype(jnp.float32)).astype(jnp.bfloat16)
             terms = jnp.concatenate([low, middle, high], axis=0)
             sums = jnp.dot(picks, terms, preferred_element_type=jnp.float32)
-            for far_y in range(FAR_Y):
-                start = (far_y * FAR_Z + far) * TILES + j
-                out[pl.ds(start, PIECES, stride=EACH), :] = sums[
-                    far_y * PIECES : (far_y + 1) * PIECES
-                ]
+            out[pl.ds(far * EACH + j, TILES, stride=FAR_Z * EACH), :] = sums
 
 
 def gather(got):
     return pl.pallas_call(
         gather_kernel,
-        out_shape=jax.ShapeDtypeStruct((PARTS * TILES, LANES), jnp.float32),
+        out_shape=jax.ShapeDtypeStruct((TILES * FAR_Z * EACH, LANES), jnp.float32),
         compiler_params=pltpu.CompilerParams(vmem_limit_bytes=SMALL),
         name="gather",
     )(got)
 
 
 def add_kernel(got, out):
-    out[...] = sum(got[pl.ds(part * TILES, TILES), :] for part in range(PARTS))
+    for far in range(FAR_Z):
+        for j in range(EACH):
+            line = far * EACH + j
+            rows = [
+                got[pl.ds(y * PIECES * FAR_Z * EACH + line, PIECES, stride=FAR_Z * EACH), :]
+                for y in range(FAR_Y)
+            ]
+            out[pl.ds(far * TILES + j, PIECES, stride=EACH), :] = sum(rows[1:], rows[0])
 
 
-def add(got):
+def finish_kernel(got, out):
+    parts = [got[pl.ds(far * TILES, TILES), :] for far in range(FAR_Z)]
+    out[...] = sum(parts[1:], parts[0])
+
+
+def add(kernel, got, rows):
     return pl.pallas_call(
-        add_kernel,
-        out_shape=jax.ShapeDtypeStruct((TILES, LANES), jnp.float32),
+        kernel,
+        out_shape=jax.ShapeDtypeStruct((rows, LANES), jnp.float32),
         compiler_params=pltpu.CompilerParams(vmem_limit_bytes=SMALL),
         name="add",
     )(got)
@@ -161,8 +168,10 @@
     sent = products(irrep_sizes, tile_slot, partners[0], amps[0], ints[0])
     got = exchange(sent, ("x", "near_y", "core", "near_z"), FIRST)
     sums = gather(got)
-    sums = add(exchange(sums, ("far_y", "far_z"), PARTS))
-    return exchange(sums, ("x", "near_y", "core"), PIECES)[None]
+    got = exchange(sums, ("far_y", "x", "near_y", "core"), TILES)
+    sums = add(add_kernel, got, FAR_Z * TILES)
+    got = exchange(sums, ("far_z",), FAR_Z)
+    return add(finish_kernel, got, TILES)[None]
 
 
 def solution(mesh):

time: 97.6 us -> 92.3 us (0.946)
  blocking collectives: 89.1 us -> 82.7 us
    all_to_all x3, blocking collectives: 89.1 us -> 82.7 us  [exchange(): return lax.all_to_all(sent, axes, 0, 0, tiled=True).reshape(rows.shape)]
where the time goes in v4:
time: 92.3 us; the launch traced here: 91.1 us
  blocking collectives  82.7 us (90%)
  Pallas kernels  8.37 us (9%)
    all_to_all x3, blocking collectives, exchange(): return lax.all_to_all(sent, axes, 0, 0, tiled=True).reshape(rows.shape)  82.7 us
    pallas_call x1, Pallas kernels, products(): pl.pallas_call(products_kernel, in_specs=[scalars] * 3 + [pl.BlockSpec(me...  6.92 us

profile of v4, /device:TPU:1, one launch (start us, length us, event | category | flops | bytes accessed | tf_op | source)
XLA Modules:
  0.0 91.1 jit_solution(17138006478461327917)
XLA Ops:
  0.0 6.9 %products.1 = f32[2352,128]{1,0:T(8,128)} custom-call(s32[2]{0:T(128)} %sizes.1, s32[64]{0:T(128)} %slots.1, s32[36]{0:T(128)} %bitcast.22, bf16[768,4096]{1,0:T(8,128)(2,1)} %bitcast.19, bf16[3,4096,128]{2,1,0:T(8,128)(2,1)} %bitcast.21), custom_call_target="tpu_custom_call" | custom-call | tf_op jit(solution)/shard_map/products/pallas_call | solution.py:91
  6.9 38.5 %all_to_all.15 = f32[48,49,1,128]{3,2,1,0:T(1,128)S(1)} all-to-all(f32[48,49,1,128]{3,2,1,0:T(1,128)} %bitcast.20), channel_id=1, replica_groups=mesh['x'=4,'far_y'=4,'near_y'=2,'core'=2,'far_z'=4,'near_z'=3] {'x','nea..., dimensions={0} | all-to-all | bytes 2408448 | tf_op jit(solution)/shard_map/all_to_all | solution.py:164
  45.5 0.7 gather.1
  46.2 20.6 %all_to_all.16 = f32[64,16,1,128]{3,1,2,0:T(8,128)S(1)} all-to-all(f32[64,16,1,128]{3,1,2,0:T(8,128)S(1)} %bitcast.16), channel_id=1, replica_groups=mesh['x'=4,'far_y'=4,'near_y'=2,'core'=2,'far_z'=4,'near_z'=3] {'far_y',..., dimensions={0} | all-to-all | bytes 1048576 | tf_op jit(solution)/shard_map/all_to_all | solution.py:164
  66.7 0.1 add.2
  66.9 23.6 %all_to_all.17 = f32[4,64,1,128]{3,1,2,0:T(8,128)S(1)} all-to-all(f32[4,64,1,128]{3,1,2,0:T(8,128)S(1)} %bitcast.17), channel_id=1, replica_groups=mesh['x'=4,'far_y'=4,'near_y'=2,'core'=2,'far_z'=4,'near_z'=3] {'far_z'}, dimensions={0} | all-to-all | bytes 262144 | tf_op jit(solution)/shard_map/all_to_all | solution.py:164
  90.5 0.6 add.3

commit v5 on v4

--- a/solution.py
+++ b/solution.py
@@ -18,7 +18,8 @@
 FIRST = PIECES * NEAR_Z
 LINES = PER * FAR_Z * EACH + 1
 LANES = 128
-CHUNK = 512
+DEPTHS = (512, 1024, 1024, 1024, 256, 256)
+STARTS = tuple(sum(DEPTHS[:step]) for step in range(len(DEPTHS)))
 HALF = 384
 ROOM = 56 * 1024 * 1024
 SMALL = 16 * 1024 * 1024
@@ -36,8 +37,8 @@
     live = jnp.where(own >= sizes[0], sizes[1], sizes[0])
     lanes = lax.broadcasted_iota(jnp.int32, (1, LANES), 1)
     far, piece = lanes // PIECES, lanes % PIECES
-    x, low = piece // (2 * NEAR_Y), piece % (2 * NEAR_Y)
-    slot_of = (x * FAR_Y + far) * 2 * NEAR_Y + low
+    x, core = piece // 2 % 4, piece % 2
+    slot_of = (x * 8 + far * NEAR_Y + piece // 8) * 2 + core
     slot_of = jnp.where(lanes < TILES, slot_of, -2)
     row = jnp.zeros((1, LANES), jnp.float32)
     for k in range(PER):
@@ -47,26 +48,34 @@
     return row
 
 
-def products_kernel(sizes, slots, partners, amps, ints, out, left, right, total, sems):
-    depth = amps.shape[1]
+def products_kernel(tables, amps, ints, out, left, right, total, held, sems, table_sems):
     copies = []
-    for step in range(depth // CHUNK):
-        part = pl.ds(step * CHUNK, CHUNK)
+    for step, (start, depth) in enumerate(zip(STARTS, DEPTHS)):
+        part = pl.ds(start, depth)
         copies.append(
             (
                 pltpu.make_async_copy(amps.at[:, part], left.at[:, part], sems.at[0, step]),
                 pltpu.make_async_copy(ints.at[:, part], right.at[:, part], sems.at[1, step]),
             )
         )
-    for pair in copies:
+    small = [
+        pltpu.make_async_copy(tables[i], held[i], table_sems.at[i]) for i in range(len(tables))
+    ]
+    for copy in copies[0]:
+        copy.start()
+    for copy in small:
+        copy.start()
+    for pair in copies[1:]:
         for copy in pair:
             copy.start()
-    row = codes_row(sizes, slots, partners)
+    for copy in small:
+        copy.wait()
+    row = codes_row(*held)
     out[pl.ds(LINES - 1, FIRST, stride=LINES), :] = jnp.broadcast_to(row, (FIRST, LANES))
     for step, pair in enumerate(copies):
         for copy in pair:
             copy.wait()
-        part = pl.ds(step * CHUNK, CHUNK)
+        part = pl.ds(STARTS[step], DEPTHS[step])
         weights = jnp.concatenate([right[k, part, :] for k in range(PER)], axis=1)
         for half in range(2):
             rows = pl.ds(half * HALF, HALF)
@@ -79,29 +88,32 @@
             for k in range(PER):
                 for j in range(EACH):
                     start = TILES * (far * NEAR_Z + near) + j
-                    line = near * LINES + (k * FAR_Z + far) * EACH + j
-                    out[pl.ds(line, PIECES, stride=NEAR_Z * LINES), :] = total[
+                    line = near * PIECES * LINES + (k * FAR_Z + far) * EACH + j
+                    out[pl.ds(line, PIECES, stride=LINES), :] = total[
                         k, pl.ds(start, PIECES, stride=EACH), :
                     ]
 
 
 def products(sizes, slots, partners, amps, ints):
     pairs, depth = amps.shape
-    scalars = pl.BlockSpec(memory_space=pltpu.SMEM)
+    anywhere = pl.BlockSpec(memory_space=pl.ANY)
+    tables = (sizes, slots, partners)
     return pl.pallas_call(
         products_kernel,
-        in_specs=[scalars] * 3 + [pl.BlockSpec(memory_space=pl.ANY)] * 2,
+        in_specs=[(anywhere,) * 3, anywhere, anywhere],
         out_specs=pl.BlockSpec(memory_space=pltpu.VMEM),
         out_shape=jax.ShapeDtypeStruct((FIRST * LINES, LANES), jnp.float32),
         scratch_shapes=[
             pltpu.VMEM((pairs, depth), jnp.bfloat16),
             pltpu.VMEM((PER, depth, LANES), jnp.bfloat16),
             pltpu.VMEM((PER, pairs, LANES), jnp.float32),
-            pltpu.SemaphoreType.DMA((2, depth // CHUNK)),
+            [pltpu.SMEM(table.shape, jnp.int32) for table in tables],
+            pltpu.SemaphoreType.DMA((2, len(DEPTHS))),
+            pltpu.SemaphoreType.DMA((len(tables),)),
         ],
         compiler_params=pltpu.CompilerParams(vmem_limit_bytes=ROOM),
         name="products",
-    )(sizes, slots, partners, amps, ints)
+    )(tables, amps, ints)
 
 
 def gather_kernel(got, out):
@@ -166,9 +178,9 @@
 
 def shards(amps, ints, partners, irrep_sizes, tile_slot):
     sent = products(irrep_sizes, tile_slot, partners[0], amps[0], ints[0])
-    got = exchange(sent, ("x", "near_y", "core", "near_z"), FIRST)
+    got = exchange(sent, ("near_z", "near_y", "x", "core"), FIRST)
     sums = gather(got)
-    got = exchange(sums, ("far_y", "x", "near_y", "core"), TILES)
+    got = exchange(sums, ("far_y", "near_y", "x", "core"), TILES)
     sums = add(add_kernel, got, FAR_Z * TILES)
     got = exchange(sums, ("far_z",), FAR_Z)
     return add(finish_kernel, got, TILES)[None]

time: 92.3 us -> 91.6 us (level)
  no operation moved by 1% of the time
where the time goes in v5:
time: 91.6 us; the launch traced here: 90.8 us
  blocking collectives  82.9 us (91%)
  Pallas kernels  7.86 us (9%)
    all_to_all x3, blocking collectives, exchange(): return lax.all_to_all(sent, axes, 0, 0, tiled=True).reshape(rows.shape)  82.9 us
    pallas_call x1, Pallas kernels, products(): pl.pallas_call(products_kernel, in_specs=[(anywhere,) * 3, anywhere, anyw...  6.41 us

profile of v5, /device:TPU:1, one launch (start us, length us, event | category | flops | bytes accessed | tf_op | source)
XLA Modules:
  0.0 90.8 jit_solution(8760867051514126180)
XLA Ops:
  0.0 6.4 %products.1 = f32[2352,128]{1,0:T(8,128)} custom-call(s32[2]{0:T(128)} %tables_0_.1, s32[64]{0:T(128)} %tables_1_.1, s32[36]{0:T(128)} %bitcast.22, bf16[768,4096]{1,0:T(8,128)(2,1)} %bitcast.19, bf16[3,4096,128]{2,1,0:T(8,128)(2,1)} %bitcast.21), custom_call_target="tpu_custom_call" | custom-call | tf_op jit(solution)/shard_map/products/pallas_call | solution.py:101
  6.4 36.9 %all_to_all.15 = f32[48,49,1,128]{3,2,1,0:T(1,128)S(1)} all-to-all(f32[48,49,1,128]{3,2,1,0:T(1,128)} %bitcast.20), channel_id=1, replica_groups=mesh['x'=4,'far_y'=4,'near_y'=2,'core'=2,'far_z'=4,'near_z'=3] {'near_z'..., dimensions={0} | all-to-all | bytes 2408448 | tf_op jit(solution)/shard_map/all_to_all | solution.py:176
  43.4 0.7 gather.1
  44.0 22.2 %all_to_all.16 = f32[64,16,1,128]{3,1,2,0:T(8,128)S(1)} all-to-all(f32[64,16,1,128]{3,1,2,0:T(8,128)S(1)} %bitcast.16), channel_id=1, replica_groups=mesh['x'=4,'far_y'=4,'near_y'=2,'core'=2,'far_z'=4,'near_z'=3] {'far_y',..., dimensions={0} | all-to-all | bytes 1048576 | tf_op jit(solution)/shard_map/all_to_all | solution.py:176
  66.2 0.1 add.2
  66.4 23.8 %all_to_all.17 = f32[4,64,1,128]{3,1,2,0:T(8,128)S(1)} all-to-all(f32[4,64,1,128]{3,1,2,0:T(8,128)S(1)} %bitcast.17), channel_id=1, replica_groups=mesh['x'=4,'far_y'=4,'near_y'=2,'core'=2,'far_z'=4,'near_z'=3] {'far_z'}, dimensions={0} | all-to-all | bytes 262144 | tf_op jit(solution)/shard_map/all_to_all | solution.py:176
  90.2 0.6 add.3

commit v6 on v5

--- a/solution.py
+++ b/solution.py
@@ -36,9 +36,7 @@
     )
     live = jnp.where(own >= sizes[0], sizes[1], sizes[0])
     lanes = lax.broadcasted_iota(jnp.int32, (1, LANES), 1)
-    far, piece = lanes // PIECES, lanes % PIECES
-    x, core = piece // 2 % 4, piece % 2
-    slot_of = (x * 8 + far * NEAR_Y + piece // 8) * 2 + core
+    slot_of = (lanes // 2 % 4 * 8 + lanes // 8) * 2 + lanes % 2
     slot_of = jnp.where(lanes < TILES, slot_of, -2)
     row = jnp.zeros((1, LANES), jnp.float32)
     for k in range(PER):
@@ -147,13 +145,13 @@
 
 def add_kernel(got, out):
     for far in range(FAR_Z):
-        for j in range(EACH):
-            line = far * EACH + j
-            rows = [
-                got[pl.ds(y * PIECES * FAR_Z * EACH + line, PIECES, stride=FAR_Z * EACH), :]
-                for y in range(FAR_Y)
-            ]
-            out[pl.ds(far * TILES + j, PIECES, stride=EACH), :] = sum(rows[1:], rows[0])
+        for near in range(NEAR_Y):
+            for j in range(EACH):
+                starts = [
+                    ((y * NEAR_Y + near) * 8 * FAR_Z + far) * EACH + j for y in range(FAR_Y)
+                ]
+                rows = [got[pl.ds(start, 8, stride=FAR_Z * EACH), :] for start in starts]
+                out[pl.ds(far * TILES + near * EACH + j, 8, stride=8), :] = sum(rows[1:], rows[0])
 
 
 def finish_kernel(got, out):
@@ -178,11 +176,11 @@
 
 def shards(amps, ints, partners, irrep_sizes, tile_slot):
     sent = products(irrep_sizes, tile_slot, partners[0], amps[0], ints[0])
-    got = exchange(sent, ("near_z", "near_y", "x", "core"), FIRST)
+    got = exchange(sent, ("near_z", "x", "core", "near_y"), FIRST)
     sums = gather(got)
-    got = exchange(sums, ("far_y", "near_y", "x", "core"), TILES)
+    got = exchange(sums, ("far_y", "near_y"), 8)
     sums = add(add_kernel, got, FAR_Z * TILES)
-    got = exchange(sums, ("far_z",), FAR_Z)
+    got = exchange(sums, ("far_z", "x", "core"), FAR_Z * 8)
     return add(finish_kernel, got, TILES)[None]
 
 

time: 91.6 us -> 93.1 us (1.016)
  blocking collectives: 82.9 us -> 84.9 us
    all_to_all x3, blocking collectives: 82.9 us -> 84.9 us  [exchange(): return lax.all_to_all(sent, axes, 0, 0, tiled=True).reshape(rows.shape)]
where the time goes in v6:
time: 93.1 us; the launch traced here: 92.8 us
  blocking collectives  84.9 us (91%)
  Pallas kernels  7.87 us (8%)
    all_to_all x3, blocking collectives, exchange(): return lax.all_to_all(sent, axes, 0, 0, tiled=True).reshape(rows.shape)  84.9 us
    pallas_call x1, Pallas kernels, products(): pl.pallas_call(products_kernel, in_specs=[(anywhere,) * 3, anywhere, anyw...  6.41 us

profile of v6, /device:TPU:1, one launch (start us, length us, event | category | flops | bytes accessed | tf_op | source)
XLA Modules:
  0.0 92.8 jit_solution(14006722251624525369)
XLA Ops:
  0.0 6.4 %products.1 = f32[2352,128]{1,0:T(8,128)} custom-call(s32[2]{0:T(128)} %tables_0_.1, s32[64]{0:T(128)} %tables_1_.1, s32[36]{0:T(128)} %bitcast.22, bf16[768,4096]{1,0:T(8,128)(2,1)} %bitcast.19, bf16[3,4096,128]{2,1,0:T(8,128)(2,1)} %bitcast.21), custom_call_target="tpu_custom_call" | custom-call | tf_op jit(solution)/shard_map/products/pallas_call | solution.py:99
  6.4 37.2 %all_to_all.15 = f32[48,49,1,128]{3,2,1,0:T(1,128)S(1)} all-to-all(f32[48,49,1,128]{3,2,1,0:T(1,128)} %bitcast.20), channel_id=1, replica_groups=mesh['x'=4,'far_y'=4,'near_y'=2,'core'=2,'far_z'=4,'near_z'=3] {'near_z'..., dimensions={0} | all-to-all | bytes 2408448 | tf_op jit(solution)/shard_map/all_to_all | solution.py:174
  43.6 0.7 gather.1
  44.3 17.5 %all_to_all.16 = f32[8,128,1,128]{3,1,2,0:T(8,128)S(1)} all-to-all(f32[8,128,1,128]{3,1,2,0:T(8,128)S(1)} %bitcast.16), channel_id=1, replica_groups=mesh['x'=4,'far_y'=4,'near_y'=2,'core'=2,'far_z'=4,'near_z'=3] {'far_y',..., dimensions={0} | all-to-all | bytes 1048576 | tf_op jit(solution)/shard_map/all_to_all | solution.py:174
  61.8 0.2 add.2
  62.0 30.2 %all_to_all.17 = f32[32,8,1,128]{3,1,2,0:T(8,128)S(1)} all-to-all(f32[32,8,1,128]{3,1,2,0:T(8,128)S(1)} %bitcast.17), channel_id=1, replica_groups=mesh['x'=4,'far_y'=4,'near_y'=2,'core'=2,'far_z'=4,'near_z'=3] {'far_z',..., dimensions={0} | all-to-all | bytes 262144 | tf_op jit(solution)/shard_map/all_to_all | solution.py:174
  92.2 0.6 add.3

commit v7 on v5

--- a/solution.py
+++ b/solution.py
@@ -36,9 +36,8 @@
     )
     live = jnp.where(own >= sizes[0], sizes[1], sizes[0])
     lanes = lax.broadcasted_iota(jnp.int32, (1, LANES), 1)
-    far, piece = lanes // PIECES, lanes % PIECES
-    x, core = piece // 2 % 4, piece % 2
-    slot_of = (x * 8 + far * NEAR_Y + piece // 8) * 2 + core
+    y = lanes % FAR_Y * NEAR_Y + lanes // FAR_Y % NEAR_Y
+    slot_of = (lanes // 8 % 4 * 8 + y) * 2 + lanes // 32
     slot_of = jnp.where(lanes < TILES, slot_of, -2)
     row = jnp.zeros((1, LANES), jnp.float32)
     for k in range(PER):
@@ -133,7 +132,9 @@
             low = (rest - middle.astype(jnp.float32)).astype(jnp.bfloat16)
             terms = jnp.concatenate([low, middle, high], axis=0)
             sums = jnp.dot(picks, terms, preferred_element_type=jnp.float32)
-            out[pl.ds(far * EACH + j, TILES, stride=FAR_Z * EACH), :] = sums
+            for core in range(2):
+                start = (core * FAR_Z + far) * 32 * EACH + j
+                out[pl.ds(start, 32, stride=EACH), :] = sums[core * 32 : core * 32 + 32]
 
 
 def gather(got):
@@ -145,20 +146,16 @@
     )(got)
 
 
-def add_kernel(got, out):
-    for far in range(FAR_Z):
+def finish_kernel(got, out):
+    half = PIECES // 2
+    for core in range(2):
         for j in range(EACH):
-            line = far * EACH + j
             rows = [
-                got[pl.ds(y * PIECES * FAR_Z * EACH + line, PIECES, stride=FAR_Z * EACH), :]
+                got[pl.ds(((core * FAR_Z + z) * half * FAR_Y + y) * EACH + j, half, stride=FAR_Y * EACH), :]
+                for z in range(FAR_Z)
                 for y in range(FAR_Y)
             ]
-            out[pl.ds(far * TILES + j, PIECES, stride=EACH), :] = sum(rows[1:], rows[0])
-
-
-def finish_kernel(got, out):
-    parts = [got[pl.ds(far * TILES, TILES), :] for far in range(FAR_Z)]
-    out[...] = sum(parts[1:], parts[0])
+            out[pl.ds(core * half * EACH + j, half, stride=EACH), :] = sum(rows[1:], rows[0])
 
 
 def add(kernel, got, rows):
@@ -178,11 +175,9 @@
 
 def shards(amps, ints, partners, irrep_sizes, tile_slot):
     sent = products(irrep_sizes, tile_slot, partners[0], amps[0], ints[0])
-    got = exchange(sent, ("near_z", "near_y", "x", "core"), FIRST)
+    got = exchange(sent, ("near_z", "core", "x", "near_y"), FIRST)
     sums = gather(got)
-    got = exchange(sums, ("far_y", "near_y", "x", "core"), TILES)
-    sums = add(add_kernel, got, FAR_Z * TILES)
-    got = exchange(sums, ("far_z",), FAR_Z)
+    got = exchange(sums, ("core", "far_z", "x", "near_y", "far_y"), TILES * FAR_Z)
     return add(finish_kernel, got, TILES)[None]
 
 

time: 91.6 us -> 94.1 us (1.027)
  blocking collectives: 82.9 us -> 86.1 us
    all_to_all x3 -> x2, blocking collectives: 82.9 us -> 86.1 us  [exchange(): return lax.all_to_all(sent, axes, 0, 0, tiled=True).reshape(rows.shape)]
where the time goes in v7:
time: 94.1 us; the launch traced here: 93.9 us
  blocking collectives  86.1 us (91%)
  Pallas kernels  7.79 us (8%)
    all_to_all x2, blocking collectives, exchange(): return lax.all_to_all(sent, axes, 0, 0, tiled=True).reshape(rows.shape)  86.1 us
    pallas_call x1, Pallas kernels, products(): pl.pallas_call(products_kernel, in_specs=[(anywhere,) * 3, anywhere, anyw...  6.41 us

profile of v7, /device:TPU:1, one launch (start us, length us, event | category | flops | bytes accessed | tf_op | source)
XLA Modules:
  0.0 93.9 jit_solution(14832734157532848253)
XLA Ops:
  0.0 6.4 %products.1 = f32[2352,128]{1,0:T(8,128)} custom-call(s32[2]{0:T(128)} %tables_0_.1, s32[64]{0:T(128)} %tables_1_.1, s32[36]{0:T(128)} %bitcast.16, bf16[768,4096]{1,0:T(8,128)(2,1)} %bitcast.13, bf16[3,4096,128]{2,1,0:T(8,128)(2,1)} %bitcast.15), custom_call_target="tpu_custom_call" | custom-call | tf_op jit(solution)/shard_map/products/pallas_call | solution.py:100
  6.4 38.5 %all_to_all.10 = f32[48,49,1,128]{3,2,1,0:T(1,128)S(1)} all-to-all(f32[48,49,1,128]{3,2,1,0:T(1,128)} %bitcast.14), channel_id=1, replica_groups=mesh['x'=4,'far_y'=4,'near_y'=2,'core'=2,'far_z'=4,'near_z'=3] {'near_z'..., dimensions={0} | all-to-all | bytes 2408448 | tf_op jit(solution)/shard_map/all_to_all | solution.py:173
  44.9 0.6 gather.1
  45.5 47.6 %all_to_all.11 = f32[256,4,1,128]{3,1,2,0:T(4,128)S(1)} all-to-all(f32[256,4,1,128]{3,1,2,0:T(4,128)S(1)} %bitcast.11), channel_id=1, replica_groups=mesh['x'=4,'far_y'=4,'near_y'=2,'core'=2,'far_z'=4,'near_z'=3] {'core','..., dimensions={0} | all-to-all | bytes 1048576 | tf_op jit(solution)/shard_map/all_to_all | solution.py:173
  93.1 0.8 add.1
